TPU v7x, 32 devices: a whole 2x2x4 slice. The times are simulated.
32 devices in a mesh: ta: 4 (over y, x), gz: 4 (over z), col: 2 (over core).
Axes of the slice: x: 2, y: 2, z: 4, core: 2. Of those that a mesh axis runs over, the one named last changes fastest.
Arguments:
- right_sides: bfloat16 [4, 2, 2, 4, 4, 8, 384], P('col', None, None, 'ta', 'gz'), may hold values from -6 to 6
- null_vectors: bfloat16 [32, 2, 2, 4, 4, 8, 384], P(None, None, None, 'ta', 'gz'), may hold values from -0.3125 to 0.3125
- coarse_op: bfloat16 [4, 4, 1, 2, 9, 64, 128], P('ta', 'gz'), may hold values from -0.1875 to 0.1875
Outputs:
- correction: float32 [4, 2, 2, 4, 4, 8, 384], P('col', None, None, 'ta', 'gz')
All inputs are finite; a program needn't handle non-finite values.
Results may differ from a plain program's by a relative error of at most 0.0054.
Values may be sent and summed in bfloat16 or wider, within the bound.
A program may use at most 64 MiB of HBM per device.

v0:
```python
import jax
import jax.numpy as jnp
from jax import lax
from jax.sharding import PartitionSpec as P


def extended(cells, sides, width):
    for axis, dim in sides:
        count = lax.axis_size(axis)
        head = lax.slice_in_dim(cells, 0, width, axis=dim)
        tail = lax.slice_in_dim(cells, cells.shape[dim] - width, cells.shape[dim], axis=dim)
        cells = jnp.concatenate(
            [
                lax.ppermute(tail, axis, [(i, (i + 1) % count) for i in range(count)]),
                cells,
                lax.ppermute(head, axis, [((i + 1) % count, i) for i in range(count)]),
            ],
            axis=dim,
        )
    return cells


def restrict_blocks(vectors, stacked):
    products = jnp.einsum(
        "kphbn,rQphbn->brQhk", vectors, stacked, preferred_element_type=jnp.float32
    )
    return products.reshape(products.shape[0], products.shape[1], -1)


def apply_coarse(coarse, operators):
    padded = extended(coarse[None, None], (("ta", 0), ("gz", 1)), 1)
    shifted = jnp.stack(
        [
            coarse,
            padded[2, 1],
            padded[0, 1],
            jnp.roll(coarse, -1, 1),
            jnp.roll(coarse, 1, 1),
            padded[1, 2],
            padded[1, 0],
            jnp.roll(coarse, -1, 0),
            jnp.roll(coarse, 1, 0),
        ]
    )
    half_width = coarse.shape[-1] // 2
    real_part = shifted[..., :half_width]
    imag_part = shifted[..., half_width:]
    stacked = jnp.stack(
        [
            jnp.concatenate([real_part, -imag_part], axis=-1),
            jnp.concatenate([imag_part, real_part], axis=-1),
        ],
        axis=-2,
    )
    result = jnp.einsum(
        "tymoc,mtyrsc->tyrso", operators, stacked, preferred_element_type=jnp.float32
    )
    return result.reshape(coarse.shape)


def prolong(vectors, coarse_rows):
    block_count = coarse_rows.shape[0] * coarse_rows.shape[1]
    rhs_count = coarse_rows.shape[2]
    vec_count = vectors.shape[0]
    halves = coarse_rows.reshape(block_count, rhs_count, 2, 2, vec_count)
    real_part = halves[:, :, 0]
    imag_part = halves[:, :, 1]
    mixing = jnp.stack(
        [jnp.stack([real_part, -imag_part], axis=2), jnp.stack([imag_part, real_part], axis=2)],
        axis=2,
    )
    result = jnp.einsum("kphbn,brPphk->rPhbn", vectors, mixing, preferred_element_type=jnp.float32)
    return result.reshape(rhs_count, 2, 2, 1, 1, block_count, -1)


def per_device(right_sides, null_vectors, coarse_op):
    xblocks = lax.axis_size("ta")
    t_blocks = coarse_op.shape[2]
    yblocks = coarse_op.shape[3]
    own_block = lax.axis_index("ta") // 4
    vectors = null_vectors[:, :, :, 0, 0]
    fields = right_sides[:, :, :, 0, 0]
    stacked = jnp.stack([fields, jnp.stack([fields[:, 1], -fields[:, 0]], axis=1)], axis=1)
    rhs_count = fields.shape[0]
    partial_value = restrict_blocks(vectors, stacked).reshape(
        1 * lax.axis_size("ta"), yblocks, rhs_count, -1
    )
    select = (jnp.arange(t_blocks) == own_block).astype(jnp.float32)
    summed = lax.psum_scatter(
        select[None, :, None, None, None] * partial_value[:, None],
        "ta",
        scatter_dimension=0,
        tiled=True,
    )
    coarse = summed.reshape(summed.shape[1:]).astype(jnp.bfloat16)
    operators = coarse_op.reshape(coarse_op.shape[2:])
    applied = apply_coarse(coarse, operators).astype(jnp.bfloat16)
    twice = apply_coarse(applied, operators).astype(jnp.bfloat16)
    gathered = lax.all_gather(twice, "ta", axis=0, tiled=True)
    arranged = gathered.reshape((xblocks, t_blocks) + twice.shape[1:])
    coarse_rows = lax.dynamic_index_in_dim(arranged, own_block, 1, keepdims=False)
    return prolong(vectors, coarse_rows)


def solution(mesh):
    return jax.shard_map(
        per_device,
        mesh=mesh,
        in_specs=(
            P("col", None, None, "ta", "gz", None, None),
            P(None, None, None, "ta", "gz", None, None),
            P("ta", "gz", None, None, None, None, None),
        ),
        out_specs=P("col", None, None, "ta", "gz", None, None),
        check_vma=False,
    )
```

profile of v0, /device:TPU:0, one launch (start us, length us, event | category | flops | bytes accessed | tf_op | source)
XLA Modules:
  0.0 50.1 jit_solution(6235054517766414990)
XLA Ops:
  0.0 0.9 %copy-done.2 = bf16[2,2,2,1,1,8,384]{6,5,4,3,2,1,0:T(8,128)(2,1)S(1)} copy-done((bf16[2,2,2,1,1,8,384]{6,5,4,3,2,1,0:T(8,128)(2,1)S(1)}, bf16[2,2,2,1,1,8,384]{6,5,4,3,2,1,0:T(8,128)(2,1)}, u32[]{:S(2)}) %copy-start.2) | copy-done | bytes 49176
  1.2 0.9 %fusion.1 = f32[8,2,2,2,32]{4,2,1,3,0:T(2,128)S(1)} fusion(bf16[32,2,2,8,384,1]{4,3,2,1,0,5:T(8,128)(2,1)S(1)} %bitcast.107, bf16[2,1,2,2,8,384]{5,1,2,0,3,4:T(2,128)(2,1)S(1)} %copy.70, bf16[2,1,2,2,8,384]{5,1,2,0,3,4:T(2,128)(2,1)S(1)} %copy.69, f32[]{:T(128)S(6)} %convert_element_type.77), kind=kOutput, calls=%fused_computation.3 | convolution fusion | flops 3344384 | bytes 892932 | tf_op jit(solution)/shard_map/kphbn,rQphbn->brQhk/dot_general | solution.py:24
  2.1 0.1 mul.25
  2.2 11.5 %all-reduce = bf16[4,1,2,2,128]{4,3,2,0,1:T(2,128)(2,1)S(1)} all-reduce(f32[4,1,2,2,128]{4,3,2,0,1:T(2,128)S(1)} %mul.25), channel_id=2, replica_groups=mesh['ta'=4,'gz'=4,'col'=2] {'ta'}, use_global_device_ids=true, to_apply=%region_0.1.clone | all-reduce | flops 2048 | bytes 12288
  13.7 0.6 %dynamic-slice.1 = u32[1]{0:T(128)} dynamic-slice(u32[32]{0:T(128)S(1)} %copy-done.3, u32[]{:T(128)S(6)} %add.6), dynamic_slice_sizes={1} | dynamic-slice | bytes 12
  14.3 0.7 %constant_dynamic-update-slice_fusion.8 = (bf16[9,1,2,2,128]{4,3,2,1,0:T(2,128)(2,1)S(1)}, bf16[1,1,2,2,128]{4,3,2,1,0:T(2,128)(2,1)S(1)}) fusion(bf16[4,1,2,2,128]{4,3,2,0,1:T(2,128)(2,1)S(1)} %all-reduce, u32[]{:T(128)} %bitcast.44), kind=kLoop, calls=%fused_computation.24 | loop fusion | bytes 3076
  15.0 0.5 collective-permute-start
  15.5 1.6 %collective-permute-start.1 = (bf16[1,1,1,2,2,128]{5,4,3,2,1,0:T(2,128)(2,1)S(1)}, bf16[1,1,1,2,2,128]{5,4,3,2,1,0:T(2,128)(2,1)S(1)}, u32[]{:S(2)}, u32[]{:S(2)}) collective-permute-start(bf16[1,1,1,2,2,128]{5,4,3,2,1,0:T(2,128)(2,1)S(1)} %bitcast.112), channel_id=1, source_target_pairs={{0,8},{8,16},{16,24},{24,0},{1,9},{9,17},{17,25},{25,1},{2,10},{10... | collective-permute-start | bytes 3080 | tf_op jit(solution)/shard_map/ppermute | solution.py:14
  17.0 1.5 %collective-permute-done = bf16[1,1,1,2,2,128]{5,4,3,2,1,0:T(2,128)(2,1)S(1)} collective-permute-done((bf16[1,1,1,2,2,128]{5,4,3,2,1,0:T(2,128)(2,1)S(1)}, bf16[1,1,1,2,2,128]{5,4,3,2,1,0:T(2,128)(2,1)S(1)}, u32[]{:S(2)}, u32[]{:S(2)}) %collective-permute-start) | collective-permute-done | bytes 1056 | tf_op jit(solution)/shard_map/ppermute | solution.py:16
  18.6 1.3 %collective-permute-done.1 = bf16[1,1,1,2,2,128]{5,4,3,2,1,0:T(2,128)(2,1)S(1)} collective-permute-done((bf16[1,1,1,2,2,128]{5,4,3,2,1,0:T(2,128)(2,1)S(1)}, bf16[1,1,1,2,2,128]{5,4,3,2,1,0:T(2,128)(2,1)S(1)}, u32[]{:S(2)}, u32[]{:S(2)}) %collective-permute-start.1) | collective-permute-done | bytes 1056 | tf_op jit(solution)/shard_map/ppermute | solution.py:14
  19.9 3.7 %collective-permute-start.2 = (bf16[3,1,1,2,2,128]{5,4,3,2,1,0:T(2,128)(2,1)S(1)}, bf16[3,1,1,2,2,128]{5,4,3,2,1,0:T(2,128)(2,1)S(1)}, u32[]{:S(2)}, u32[]{:S(2)}) collective-permute-start(bf16[3,1,1,2,2,128]{5,4,3,2,1,0:T(2,128)(2,1)S(1)} %pad_maximum_fusion), channel_id=1, source_target_pairs={{2,0},{4,2},{6,4},{0,6},{3,1},{5,3},{7,5},{1,7},{10,8},{12,10},{14... | collective-permute-start | bytes 9224 | tf_op jit(solution)/shard_map/ppermute | solution.py:16
  23.6 1.3 %collective-permute-done.2 = bf16[3,1,1,2,2,128]{5,4,3,2,1,0:T(2,128)(2,1)S(1)} collective-permute-done((bf16[3,1,1,2,2,128]{5,4,3,2,1,0:T(2,128)(2,1)S(1)}, bf16[3,1,1,2,2,128]{5,4,3,2,1,0:T(2,128)(2,1)S(1)}, u32[]{:S(2)}, u32[]{:S(2)}) %collective-permute-start.2) | collective-permute-done | bytes 3104 | tf_op jit(solution)/shard_map/ppermute | solution.py:16
  24.9 4.1 %collective-permute-done.3 = bf16[3,1,1,2,2,128]{5,4,3,2,1,0:T(2,128)(2,1)S(1)} collective-permute-done((bf16[3,1,1,2,2,128]{5,4,3,2,1,0:T(2,128)(2,1)S(1)}, bf16[3,1,1,2,2,128]{5,4,3,2,1,0:T(2,128)(2,1)S(1)}, u32[]{:S(2)}, u32[]{:S(2)}) %collective-permute-start.3) | collective-permute-done | bytes 3104 | tf_op jit(solution)/shard_map/ppermute | solution.py:14
  29.3 0.2 fusion.2
  29.6 0.7 %collective-permute-start.5 = (bf16[1,1,1,2,2,128]{5,4,3,2,1,0:T(2,128)(2,1)S(1)}, bf16[1,1,1,2,2,128]{5,4,3,2,1,0:T(2,128)(2,1)S(1)}, u32[]{:S(2)}, u32[]{:S(2)}) collective-permute-start(bf16[1,1,1,2,2,128]{5,4,3,2,1,0:T(2,128)(2,1)S(1)} %convert_element_type.83), channel_id=1, source_target_pairs={{0,8},{8,16},{16,24},{24,0},{1,9},{9,17},{17,25},{25,1},{2,10},{10... | collective-permute-start | bytes 3080 | tf_op jit(solution)/shard_map/ppermute | solution.py:14
  30.3 2.2 %collective-permute-start.4 = (bf16[1,1,1,2,2,128]{5,4,3,2,1,0:T(2,128)(2,1)S(1)}, bf16[1,1,1,2,2,128]{5,4,3,2,1,0:T(2,128)(2,1)S(1)}, u32[]{:S(2)}, u32[]{:S(2)}) collective-permute-start(bf16[1,1,1,2,2,128]{5,4,3,2,1,0:T(2,128)(2,1)S(1)} %convert_element_type.83), channel_id=1, source_target_pairs={{8,0},{16,8},{24,16},{0,24},{9,1},{17,9},{25,17},{1,25},{10,2},{18... | collective-permute-start | bytes 3080 | tf_op jit(solution)/shard_map/ppermute | solution.py:16
  32.7 1.4 %collective-permute-done.5 = bf16[1,1,1,2,2,128]{5,4,3,2,1,0:T(2,128)(2,1)S(1)} collective-permute-done((bf16[1,1,1,2,2,128]{5,4,3,2,1,0:T(2,128)(2,1)S(1)}, bf16[1,1,1,2,2,128]{5,4,3,2,1,0:T(2,128)(2,1)S(1)}, u32[]{:S(2)}, u32[]{:S(2)}) %collective-permute-start.5) | collective-permute-done | bytes 1056 | tf_op jit(solution)/shard_map/ppermute | solution.py:14
  34.2 2.0 %collective-permute-start.7 = (bf16[3,1,1,2,2,128]{5,4,3,2,1,0:T(2,128)(2,1)S(1)}, bf16[3,1,1,2,2,128]{5,4,3,2,1,0:T(2,128)(2,1)S(1)}, u32[]{:S(2)}, u32[]{:S(2)}) collective-permute-start(bf16[3,1,1,2,2,128]{5,4,3,2,1,0:T(2,128)(2,1)S(1)} %constant_dynamic-update-slice_fusion.9), channel_id=1, source_target_pairs={{0,2},{2,4},{4,6},{6,0},{1,3},{3,5},{5,7},{7,1},{8,10},{10,12},{12... | collective-permute-start | bytes 9224 | tf_op jit(solution)/shard_map/ppermute | solution.py:14
  36.2 1.5 %collective-permute-done.6 = bf16[3,1,1,2,2,128]{5,4,3,2,1,0:T(2,128)(2,1)S(1)} collective-permute-done((bf16[3,1,1,2,2,128]{5,4,3,2,1,0:T(2,128)(2,1)S(1)}, bf16[3,1,1,2,2,128]{5,4,3,2,1,0:T(2,128)(2,1)S(1)}, u32[]{:S(2)}, u32[]{:S(2)}) %collective-permute-start.6) | collective-permute-done | bytes 3104 | tf_op jit(solution)/shard_map/ppermute | solution.py:16
  37.8 1.9 %collective-permute-done.7 = bf16[3,1,1,2,2,128]{5,4,3,2,1,0:T(2,128)(2,1)S(1)} collective-permute-done((bf16[3,1,1,2,2,128]{5,4,3,2,1,0:T(2,128)(2,1)S(1)}, bf16[3,1,1,2,2,128]{5,4,3,2,1,0:T(2,128)(2,1)S(1)}, u32[]{:S(2)}, u32[]{:S(2)}) %collective-permute-start.7) | collective-permute-done | bytes 3104 | tf_op jit(solution)/shard_map/ppermute | solution.py:14
  39.9 0.2 fusion.3
  40.2 8.6 %all_gather.3 = bf16[4,2,2,128]{3,2,1,0:T(2,128)(2,1)S(1)} all-gather(bf16[1,2,2,128]{3,2,1,0:T(2,128)(2,1)S(1)} %convert_element_type.86), channel_id=1, replica_groups=mesh['ta'=4,'gz'=4,'col'=2] {'ta'}, dimensions={0}, use_global_device_ids=true | all-gather | bytes 5120 | tf_op jit(solution)/shard_map/all_gather | solution.py:99
  49.0 0.5 convolution_bitcast_fusion
  49.5 0.7 %copy.83 = f32[2,2,2,1,1,8,384]{6,5,4,3,2,1,0:T(8,128)} copy(f32[2,2,2,1,1,8,384]{6,1,0,5,2,4,3:T(2,128)S(1)} %convolution_bitcast_fusion) | data formatting | bytes 196608 | tf_op jit(solution)/shard_map/reshape | solution.py:73
  (55 shorter events, 1.6 us)
Async XLA Ops:
  0.0 1.2 %copy-start = (bf16[32,2,2,1,1,8,384]{6,5,4,3,2,1,0:T(8,128)(2,1)S(1)}, bf16[32,2,2,1,1,8,384]{6,5,4,3,2,1,0:T(8,128)(2,1)}, u32[]{:S(2)}) copy-start(bf16[32,2,2,1,1,8,384]{6,5,4,3,2,1,0:T(8,128)(2,1)} %param.4) | copy-start | bytes 2359300
  0.0 0.9 %copy-start.2 = (bf16[2,2,2,1,1,8,384]{6,5,4,3,2,1,0:T(8,128)(2,1)S(1)}, bf16[2,2,2,1,1,8,384]{6,5,4,3,2,1,0:T(8,128)(2,1)}, u32[]{:S(2)}) copy-start(bf16[2,2,2,1,1,8,384]{6,5,4,3,2,1,0:T(8,128)(2,1)} %param.3) | copy-start | bytes 147460
  1.2 12.5 %copy-start.3 = (u32[32]{0:T(128)S(1)}, u32[32]{0:T(128)}, u32[]{:S(2)}) copy-start(u32[32]{0:T(128)} %constant.32) | copy-start | bytes 388
  2.1 27.2 %copy-start.1 = (bf16[1,1,1,2,9,64,128]{6,5,4,3,2,1,0:T(8,128)(2,1)S(1)}, bf16[1,1,1,2,9,64,128]{6,5,4,3,2,1,0:T(8,128)(2,1)}, u32[]{:S(2)}) copy-start(bf16[1,1,1,2,9,64,128]{6,5,4,3,2,1,0:T(8,128)(2,1)} %param.5) | copy-start | bytes 884740
  15.0 3.6 %collective-permute-start = (bf16[1,1,1,2,2,128]{5,4,3,2,1,0:T(2,128)(2,1)S(1)}, bf16[1,1,1,2,2,128]{5,4,3,2,1,0:T(2,128)(2,1)S(1)}, u32[]{:S(2)}, u32[]{:S(2)}) collective-permute-start(bf16[1,1,1,2,2,128]{5,4,3,2,1,0:T(2,128)(2,1)S(1)} %bitcast.111), channel_id=1, source_target_pairs={{8,0},{16,8},{24,16},{0,24},{9,1},{17,9},{25,17},{1,25},{10,2},{18... | collective-permute-start | bytes 3080 | tf_op jit(solution)/shard_map/ppermute | solution.py:16
  15.5 4.5 %collective-permute-start.1 = (bf16[1,1,1,2,2,128]{5,4,3,2,1,0:T(2,128)(2,1)S(1)}, bf16[1,1,1,2,2,128]{5,4,3,2,1,0:T(2,128)(2,1)S(1)}, u32[]{:S(2)}, u32[]{:S(2)}) collective-permute-start(bf16[1,1,1,2,2,128]{5,4,3,2,1,0:T(2,128)(2,1)S(1)} %bitcast.112), channel_id=1, source_target_pairs={{0,8},{8,16},{16,24},{24,0},{1,9},{9,17},{17,25},{25,1},{2,10},{10... | collective-permute-start | bytes 3080 | tf_op jit(solution)/shard_map/ppermute | solution.py:14
  19.9 5.0 %collective-permute-start.2 = (bf16[3,1,1,2,2,128]{5,4,3,2,1,0:T(2,128)(2,1)S(1)}, bf16[3,1,1,2,2,128]{5,4,3,2,1,0:T(2,128)(2,1)S(1)}, u32[]{:S(2)}, u32[]{:S(2)}) collective-permute-start(bf16[3,1,1,2,2,128]{5,4,3,2,1,0:T(2,128)(2,1)S(1)} %pad_maximum_fusion), channel_id=1, source_target_pairs={{2,0},{4,2},{6,4},{0,6},{3,1},{5,3},{7,5},{1,7},{10,8},{12,10},{14... | collective-permute-start | bytes 9224 | tf_op jit(solution)/shard_map/ppermute | solution.py:16
  23.6 5.4 %collective-permute-start.3 = (bf16[3,1,1,2,2,128]{5,4,3,2,1,0:T(2,128)(2,1)S(1)}, bf16[3,1,1,2,2,128]{5,4,3,2,1,0:T(2,128)(2,1)S(1)}, u32[]{:S(2)}, u32[]{:S(2)}) collective-permute-start(bf16[3,1,1,2,2,128]{5,4,3,2,1,0:T(2,128)(2,1)S(1)} %pad_maximum_fusion), channel_id=1, source_target_pairs={{0,2},{2,4},{4,6},{6,0},{1,3},{3,5},{5,7},{7,1},{8,10},{10,12},{12... | collective-permute-start | bytes 9224 | tf_op jit(solution)/shard_map/ppermute | solution.py:14
  29.6 4.5 %collective-permute-start.5 = (bf16[1,1,1,2,2,128]{5,4,3,2,1,0:T(2,128)(2,1)S(1)}, bf16[1,1,1,2,2,128]{5,4,3,2,1,0:T(2,128)(2,1)S(1)}, u32[]{:S(2)}, u32[]{:S(2)}) collective-permute-start(bf16[1,1,1,2,2,128]{5,4,3,2,1,0:T(2,128)(2,1)S(1)} %convert_element_type.83), channel_id=1, source_target_pairs={{0,8},{8,16},{16,24},{24,0},{1,9},{9,17},{17,25},{25,1},{2,10},{10... | collective-permute-start | bytes 3080 | tf_op jit(solution)/shard_map/ppermute | solution.py:14
  30.3 3.8 %collective-permute-start.4 = (bf16[1,1,1,2,2,128]{5,4,3,2,1,0:T(2,128)(2,1)S(1)}, bf16[1,1,1,2,2,128]{5,4,3,2,1,0:T(2,128)(2,1)S(1)}, u32[]{:S(2)}, u32[]{:S(2)}) collective-permute-start(bf16[1,1,1,2,2,128]{5,4,3,2,1,0:T(2,128)(2,1)S(1)} %convert_element_type.83), channel_id=1, source_target_pairs={{8,0},{16,8},{24,16},{0,24},{9,1},{17,9},{25,17},{1,25},{10,2},{18... | collective-permute-start | bytes 3080 | tf_op jit(solution)/shard_map/ppermute | solution.py:16
  34.1 3.6 %collective-permute-start.6 = (bf16[3,1,1,2,2,128]{5,4,3,2,1,0:T(2,128)(2,1)S(1)}, bf16[3,1,1,2,2,128]{5,4,3,2,1,0:T(2,128)(2,1)S(1)}, u32[]{:S(2)}, u32[]{:S(2)}) collective-permute-start(bf16[3,1,1,2,2,128]{5,4,3,2,1,0:T(2,128)(2,1)S(1)} %constant_dynamic-update-slice_fusion.9), channel_id=1, source_target_pairs={{2,0},{4,2},{6,4},{0,6},{3,1},{5,3},{7,5},{1,7},{10,8},{12,10},{14... | collective-permute-start | bytes 9224 | tf_op jit(solution)/shard_map/ppermute | solution.py:16
  34.2 5.4 %collective-permute-start.7 = (bf16[3,1,1,2,2,128]{5,4,3,2,1,0:T(2,128)(2,1)S(1)}, bf16[3,1,1,2,2,128]{5,4,3,2,1,0:T(2,128)(2,1)S(1)}, u32[]{:S(2)}, u32[]{:S(2)}) collective-permute-start(bf16[3,1,1,2,2,128]{5,4,3,2,1,0:T(2,128)(2,1)S(1)} %constant_dynamic-update-slice_fusion.9), channel_id=1, source_target_pairs={{0,2},{2,4},{4,6},{6,0},{1,3},{3,5},{5,7},{7,1},{8,10},{10,12},{12... | collective-permute-start | bytes 9224 | tf_op jit(solution)/shard_map/ppermute | solution.py:14
where the time goes:
time: 50.4 us; the launch traced here: 50.1 us
  blocking collectives  20.1 us (40%)
  waiting for transfers between devices  13 us (26%)
  starting transfers between devices  10.8 us (21%)
  local copies, waits for them, and re-layouts  3.83 us (8%)
  matrix products  1.82 us (4%)
  other arithmetic  0.52 us (1%)
    unnamed x1, blocking collectives  11.5 us
    ppermute x4, waiting for transfers between devices, extended(): lax.ppermute(tail, axis, [(i, (i + 1) % count) for i in range(count)])  8.63 us
    all_gather x1, blocking collectives, per_device(): gathered = lax.all_gather(twice, 'ta', axis=0, tiled=True)  8.57 us
    ppermute x4, starting transfers between devices, extended(): lax.ppermute(head, axis, [((i + 1) % count, i) for i in range(count)])  6.47 us
    ppermute x4, waiting for transfers between devices, extended(): lax.ppermute(head, axis, [((i + 1) % count, i) for i in range(count)])  4.34 us
    ppermute x4, starting transfers between devices, extended(): lax.ppermute(tail, axis, [(i, (i + 1) % count) for i in range(count)])  4.28 us
    unnamed x23, local copies, waits for them, and re-layouts  2.33 us
  transfers between devices with their start and end apart: 8, of which 7 were waited for; matrix products, arithmetic and copies ran while one was open for 1% of the time, Pallas kernels for 0%

commit v1 on v0

v1 whole, which is shorter than its diff:
```python
import functools

import jax
import jax.numpy as jnp
from jax import lax
from jax.experimental import pallas as pl
from jax.experimental.pallas import tpu as pltpu
from jax.sharding import PartitionSpec as P

TSITES = 4
MESH = pl.DeviceIdType.MESH
F32 = jnp.float32
BF16 = jnp.bfloat16
NN = (((1,), (0,)), ((), ()))
NT = (((1,), (1,)), ((), ()))


def dot(a, b, dims):
    return lax.dot_general(a, b, dims, preferred_element_type=F32)


def same_block(rows, lanes, row_period):
    i = lax.broadcasted_iota(jnp.int32, (rows, lanes), 0)
    j = lax.broadcasted_iota(jnp.int32, (rows, lanes), 1)
    return ((i ^ j) & (row_period - 1)) == 0


def kernel(
    dims, fields_hbm, vectors_hbm, ops_hbm, out_ref,
    fields, vectors, ops, fold, spread, ext, matrix, recv, recvz, mine, halo, final, gath,
    load_sem, send1, recv1, sendz, recvz_sem, send2, recv2, send3, recv3,
):
    nx, nz, nt, ny, nr, nv, nb, chunk = dims
    me = lax.axis_index("ta")
    z = lax.axis_index("gz")
    col = lax.axis_index("col")
    up = lax.rem(z + 1, nz)
    down = lax.rem(z + nz - 1, nz)
    shift = nb.bit_length() - 1
    vec_rows = vectors.shape[0]
    rows = fields.shape[0]

    load_f = pltpu.make_async_copy(fields_hbm, fields, load_sem.at[0])
    load_v = pltpu.make_async_copy(vectors_hbm, vectors, load_sem.at[1])
    load_o = pltpu.make_async_copy(ops_hbm, ops, load_sem.at[2])
    load_f.start()
    load_v.start()
    load_o.start()

    barrier = pltpu.get_barrier_semaphore()
    for d in range(nx):
        other = lax.rem(me + d, nx)
        for plane in (up, down) if d == 0 else (up, down, z):
            pl.semaphore_signal(
                barrier, inc=1, device_id=(other, plane, col), device_id_type=MESH
            )

    i = lax.broadcasted_iota(jnp.int32, (vec_rows, 128), 0)
    j = lax.broadcasted_iota(jnp.int32, (vec_rows, 128), 1)
    lane_of = ((i >> shift) & 3) * nv + (i >> (shift + 2))
    fold[...] = jnp.where(lane_of == j, 1.0, 0.0).astype(BF16)
    i = lax.broadcasted_iota(jnp.int32, (128, vec_rows), 1)
    j = lax.broadcasted_iota(jnp.int32, (128, vec_rows), 0)
    lane_of = ((i >> shift) & 3) * nv + (i >> (shift + 2))
    spread[...] = jnp.where(lane_of == j, 1.0, 0.0).astype(BF16)

    load_f.wait()
    load_v.wait()

    mask = same_block(rows, chunk, 2 * nb)
    left = fields[...]
    total = jnp.zeros((rows, 128), F32)
    for c in range(vec_rows // chunk):
        part = pl.ds(c * chunk, chunk)
        grid = jnp.where(mask, dot(left, vectors[part, :], NT), 0.0)
        high = grid.astype(BF16)
        low = (grid - high.astype(F32)).astype(BF16)
        both = dot(jnp.concatenate([high, low], axis=0), fold[part, :], NN)
        total = total + (both[:rows] + both[rows:])
    lane = lax.broadcasted_iota(jnp.int32, (nb, 128), 1)
    sign = jnp.where(lane < 64, 1.0, -1.0)
    for r in range(nr):
        block = [total[(r * 4 + q) * nb:(r * 4 + q + 1) * nb] for q in range(4)]
        coarse = sign * (block[0] + block[1]) + pltpu.roll(block[2] + block[3], 64, 1)
        for x in range(nx):
            ext[x + 1, r * ny:(r + 1) * ny, :] = coarse[x * ny:(x + 1) * ny]
        ext[0, r * ny:(r + 1) * ny, :] = coarse[(nx - 1) * ny:]
        ext[nx + 1, r * ny:(r + 1) * ny, :] = coarse[:ny]

    pl.semaphore_wait(barrier, 3 * nx - 1)
    sends = []
    for d in range(nx):
        other = lax.rem(me + d, nx)
        for side, plane in ((1, up), (0, down)):
            sends.append(
                pltpu.make_async_remote_copy(
                    src_ref=ext.at[other + 1],
                    dst_ref=recvz.at[side, me],
                    send_sem=sendz.at[side, d],
                    recv_sem=recvz_sem.at[side, d],
                    device_id=(other, plane, col),
                    device_id_type=MESH,
                )
            )
            sends[-1].start()
        if d > 0:
            sends.append(
                pltpu.make_async_remote_copy(
                    src_ref=ext.at[pl.ds(other, 3)],
                    dst_ref=recv.at[me],
                    send_sem=send1.at[d],
                    recv_sem=recv1.at[d],
                    device_id=(other, z, col),
                    device_id_type=MESH,
                )
            )
            sends[-1].start()
    recv[pl.ds(me, 1)] = ext[pl.ds(me, 3)][None]

    load_o.wait()
    lane = lax.broadcasted_iota(jnp.int32, (64, 128), 1)
    sign64 = jnp.where(lane < 64, 1.0, -1.0)
    for t in range(nt):
        for y in range(ny):
            for m in range(9):
                a = ops[t * ny + y, m].astype(F32)
                cols = pl.ds(m * 128, 128)
                matrix[t, y * 128:y * 128 + 64, cols] = (a * sign64).astype(BF16)
                matrix[t, y * 128 + 64:y * 128 + 128, cols] = pltpu.roll(a, 64, 1).astype(BF16)

    site = lax.broadcasted_iota(jnp.int32, (nr * ny, 128), 0)

    def roll_y(v, step):
        pieces = []
        for r in range(nr):
            for y in range(ny):
                row = r * ny + (y + step) % ny
                pieces.append(v[row:row + 1])
        return jnp.concatenate(pieces, axis=0)

    def apply(own, xp, xm, zp, zm):
        results = []
        for t in range(nt):
            v = own[t]
            yp, ym = roll_y(v, 1), roll_y(v, -1)
            around = jnp.concatenate(
                [v, xp[t], xm[t], yp, ym, zp[t], zm[t], own[(t + 1) % nt], own[(t - 1) % nt]],
                axis=1,
            )
            product = dot(around.astype(BF16), matrix[t], NT)
            value = product[:, :128]
            for y in range(1, ny):
                value = jnp.where(
                    lax.rem(site, ny) == y, product[:, y * 128:(y + 1) * 128], value
                )
            results.append(value.astype(BF16).astype(F32))
        return results

    for copy in sends:
        copy.wait_recv()

    def summed(load):
        results = []
        for t in range(nt):
            value = load(t * TSITES)
            for s in range(1, TSITES):
                value = value + load(t * TSITES + s)
            results.append(value.astype(BF16).astype(F32))
        return results

    applied = apply(
        summed(lambda s: recv[s, 1]),
        summed(lambda s: recv[s, 2]),
        summed(lambda s: recv[s, 0]),
        summed(lambda s: recvz[0, s]),
        summed(lambda s: recvz[1, s]),
    )
    for t in range(nt):
        mine[t] = applied[t]

    right = lax.rem(me + 1, nx)
    left_x = lax.rem(me + nx - 1, nx)
    places = ((1, (right, z)), (0, (left_x, z)), (3, (me, up)), (2, (me, down)))
    round2 = []
    for slot, place in places:
        round2.append(
            pltpu.make_async_remote_copy(
                src_ref=mine,
                dst_ref=halo.at[slot],
                send_sem=send2.at[slot],
                recv_sem=recv2.at[slot],
                device_id=place + (col,),
                device_id_type=MESH,
            )
        )
        round2[-1].start()
    for copy in sends:
        copy.wait_send()
    for copy in round2:
        copy.wait_recv()
    twice = apply(
        applied, *[[halo[slot, t] for t in range(nt)] for slot in range(4)]
    )
    for t in range(nt):
        final[t] = twice[t]

    round3 = []
    for d in range(1, nx):
        other = lax.rem(me + d, nx)
        round3.append(
            pltpu.make_async_remote_copy(
                src_ref=final.at[other // TSITES],
                dst_ref=gath.at[me],
                send_sem=send3.at[d],
                recv_sem=recv3.at[d],
                device_id=(other, z, col),
                device_id_type=MESH,
            )
        )
        round3[-1].start()
    gath[pl.ds(me, 1)] = final[pl.ds(me // TSITES, 1)]
    for copy in round2:
        copy.wait_send()
    for copy in round3:
        copy.wait_recv()

    pieces = []
    for r in range(nr):
        row = jnp.concatenate([gath[x, r * ny:(r + 1) * ny, :] for x in range(nx)], axis=0)
        real = sign * row
        imag = pltpu.roll(row, 64, 1)
        pieces += [real, real, imag, imag]
    mixing = jnp.concatenate(pieces, axis=0).astype(BF16)
    result = None
    for c in range(vec_rows // chunk):
        part = pl.ds(c * chunk, chunk)
        weights = jnp.where(mask, dot(mixing, spread[:, part], NN), 0.0).astype(BF16)
        term = dot(weights, vectors[part, :], NN)
        result = term if result is None else result + term
    out_ref[...] = result
    for copy in round3:
        copy.wait_send()


def per_device(right_sides, null_vectors, coarse_op):
    nx = lax.axis_size("ta")
    nz = lax.axis_size("gz")
    nt, ny = coarse_op.shape[2:4]
    nr = right_sides.shape[0]
    nv = null_vectors.shape[0]
    nb, width = null_vectors.shape[-2:]
    vec_rows = nv * 4 * nb
    rows = nr * 4 * nb
    message = (nr * ny, 128)
    dma = pltpu.SemaphoreType.DMA
    out = pl.pallas_call(
        functools.partial(kernel, (nx, nz, nt, ny, nr, nv, nb, min(vec_rows, 1024))),
        out_shape=jax.ShapeDtypeStruct((rows, width), F32),
        in_specs=[pl.BlockSpec(memory_space=pl.ANY)] * 3,
        out_specs=pl.BlockSpec(memory_space=pltpu.VMEM),
        scratch_shapes=[
            pltpu.VMEM((rows, width), BF16),
            pltpu.VMEM((vec_rows, width), BF16),
            pltpu.VMEM((nt * ny, 9, 64, 128), BF16),
            pltpu.VMEM((vec_rows, 128), BF16),
            pltpu.VMEM((128, vec_rows), BF16),
            pltpu.VMEM((nx + 2,) + message, F32),
            pltpu.VMEM((nt, ny * 128, 9 * 128), BF16),
            pltpu.VMEM((nx, 3) + message, F32),
            pltpu.VMEM((2, nx) + message, F32),
            pltpu.VMEM((nt,) + message, F32),
            pltpu.VMEM((4, nt) + message, F32),
            pltpu.VMEM((nt,) + message, F32),
            pltpu.VMEM((nx,) + message, F32),
            dma((3,)),
            dma((nx,)),
            dma((nx,)),
            dma((2, nx)),
            dma((2, nx)),
            dma((4,)),
            dma((4,)),
            dma((nx,)),
            dma((nx,)),
        ],
        compiler_params=pltpu.CompilerParams(
            collective_id=0, has_side_effects=True, vmem_limit_bytes=40 * 1024 * 1024
        ),
    )(
        right_sides.reshape(rows, width),
        null_vectors.reshape(vec_rows, width),
        coarse_op.reshape((nt * ny,) + coarse_op.shape[4:]),
    )
    return out.reshape(right_sides.shape)


def solution(mesh):
    return jax.shard_map(
        per_device,
        mesh=mesh,
        in_specs=(
            P("col", None, None, "ta", "gz", None, None),
            P(None, None, None, "ta", "gz", None, None),
            P("ta", "gz", None, None, None, None, None),
        ),
        out_specs=P("col", None, None, "ta", "gz", None, None),
        check_vma=False,
    )
```

time: 50.4 us -> 23.6 us (0.47)
  blocking collectives: 20.1 us -> 0 us
  Pallas kernels: 0 us -> 19.8 us
  waiting for transfers between devices: 13 us -> 0 us
  starting transfers between devices: 10.8 us -> 0 us
  matrix products: 1.82 us -> 0 us
  other arithmetic: 0.52 us -> 0 us
    pallas_call x0 -> x1, Pallas kernels: none -> 19.8 us  [per_device(): pl.pallas_call(functools.partial(kernel, (nx, nz, nt, ny, nr, nv, nb, min...]
    ppermute x8 -> x0, waiting for transfers between devices: 13 us -> none  [the longest x4 8.63 us: extended(): lax.ppermute(tail, axis, [(i, (i + 1) % count) for i in range(count)])]
    unnamed x1 -> x0, blocking collectives: 11.5 us -> none
    ppermute x8 -> x0, starting transfers between devices: 10.8 us -> none  [the longest x4 6.47 us: extended(): lax.ppermute(head, axis, [((i + 1) % count, i) for i in range(count)])]
    all_gather x1 -> x0, blocking collectives: 8.57 us -> none  [per_device(): gathered = lax.all_gather(twice, 'ta', axis=0, tiled=True)]
    dot_general x4 -> x0, matrix products: 1.82 us -> none  [the longest x1 0.89 us: restrict_blocks(): jnp.einsum('kphbn,rQphbn->brQhk', vectors, stacked, preferred_element_typ...]
    unnamed x23 -> x7, local copies, waits for them, and re-layouts: 2.33 us -> 3.53 us
    reshape x2 -> x0, local copies, waits for them, and re-layouts: 0.73 us -> none  [the longest x1 0.65 us: prolong(): return result.reshape(rhs_count, 2, 2, 1, 1, block_count, -1)]
  transfers between devices with their start and end apart: 8 -> 0, of which waited for: 7 -> 0; matrix products, arithmetic and copies ran while one was open for 1% -> 0% of each run, Pallas kernels for 0% -> 0%
where the time goes in v1:
time: 23.6 us; the launch traced here: 23.3 us
  Pallas kernels  19.8 us (84%)
  local copies, waits for them, and re-layouts  3.53 us (15%)
    pallas_call x1, Pallas kernels, per_device(): pl.pallas_call(functools.partial(kernel, (nx, nz, nt, ny, nr, nv, nb, min...  19.8 us
    unnamed x7, local copies, waits for them, and re-layouts  3.53 us

profile of v1, /device:TPU:0, one launch (start us, length us, event | category | flops | bytes accessed | tf_op | source)
XLA Modules:
  0.0 23.3 jit_solution(15597907422918763532)
XLA Ops:
  0.0 0.0 copy-start
  0.0 1.1 %copy-done = bf16[32,2,2,1,1,8,384]{6,5,4,3,2,1,0:T(8,128)(2,1)S(1)} copy-done((bf16[32,2,2,1,1,8,384]{6,5,4,3,2,1,0:T(8,128)(2,1)S(1)}, bf16[32,2,2,1,1,8,384]{6,5,4,3,2,1,0:T(8,128)(2,1)}, u32[]{:S(2)}) %copy-start) | copy-done | bytes 786456
  1.1 0.0 copy-start.1
  1.1 1.0 %copy-done.1 = bf16[1,1,1,2,9,64,128]{6,5,4,3,2,1,0:T(8,128)(2,1)S(1)} copy-done((bf16[1,1,1,2,9,64,128]{6,5,4,3,2,1,0:T(8,128)(2,1)S(1)}, bf16[1,1,1,2,9,64,128]{6,5,4,3,2,1,0:T(8,128)(2,1)}, u32[]{:S(2)}) %copy-start.1) | copy-done | bytes 294936
  2.1 0.0 copy-start.2
  2.1 0.8 %copy-done.2 = bf16[2,2,2,1,1,8,384]{6,5,4,3,2,1,0:T(8,128)(2,1)S(1)} copy-done((bf16[2,2,2,1,1,8,384]{6,5,4,3,2,1,0:T(8,128)(2,1)S(1)}, bf16[2,2,2,1,1,8,384]{6,5,4,3,2,1,0:T(8,128)(2,1)}, u32[]{:S(2)}) %copy-start.2) | copy-done | bytes 49176
  2.9 19.8 %shard_map.37 = f32[64,384]{1,0:T(8,128)S(1)} custom-call(bf16[64,384]{1,0:T(8,128)(2,1)S(1)} %bitcast.9, bf16[1024,384]{1,0:T(8,128)(2,1)S(1)} %bitcast.6, bf16[2,9,64,128]{3,2,1,0:T(8,128)(2,1)S(1)} %bitcast.8), custom_call_target="tpu_custom_call" | custom-call | tf_op jit(solution)/shard_map/pallas_call | solution.py:256
  22.7 0.6 %copy.6 = f32[2,2,2,1,1,8,384]{6,5,4,3,2,1,0:T(8,128)} copy(f32[2,2,2,1,1,8,384]{6,5,4,3,2,1,0:T(8,128)S(1)} %bitcast.7) | data formatting | bytes 196608
Async XLA Ops:
  0.0 1.1 %copy-start = (bf16[32,2,2,1,1,8,384]{6,5,4,3,2,1,0:T(8,128)(2,1)S(1)}, bf16[32,2,2,1,1,8,384]{6,5,4,3,2,1,0:T(8,128)(2,1)}, u32[]{:S(2)}) copy-start(bf16[32,2,2,1,1,8,384]{6,5,4,3,2,1,0:T(8,128)(2,1)} %param.4) | copy-start | bytes 2359300
  1.1 1.0 %copy-start.1 = (bf16[1,1,1,2,9,64,128]{6,5,4,3,2,1,0:T(8,128)(2,1)S(1)}, bf16[1,1,1,2,9,64,128]{6,5,4,3,2,1,0:T(8,128)(2,1)}, u32[]{:S(2)}) copy-start(bf16[1,1,1,2,9,64,128]{6,5,4,3,2,1,0:T(8,128)(2,1)} %param.5) | copy-start | bytes 884740
  2.1 0.8 %copy-start.2 = (bf16[2,2,2,1,1,8,384]{6,5,4,3,2,1,0:T(8,128)(2,1)S(1)}, bf16[2,2,2,1,1,8,384]{6,5,4,3,2,1,0:T(8,128)(2,1)}, u32[]{:S(2)}) copy-start(bf16[2,2,2,1,1,8,384]{6,5,4,3,2,1,0:T(8,128)(2,1)} %param.3) | copy-start | bytes 147460

commit v2 on v1

--- a/solution.py
+++ b/solution.py
@@ -13,6 +13,7 @@
 BF16 = jnp.bfloat16
 NN = (((1,), (0,)), ((), ()))
 NT = (((1,), (1,)), ((), ()))
+ORDER = (0, 3, 4, 7, 8, 1, 2, 5, 6)
 
 
 def dot(a, b, dims):
@@ -27,7 +28,7 @@
 
 def kernel(
     dims, fields_hbm, vectors_hbm, ops_hbm, out_ref,
-    fields, vectors, ops, fold, spread, ext, matrix, recv, recvz, mine, halo, final, gath,
+    fields, vectors, ops, fold, ext, matrix, recv, recvz, mine, halo, final, gath, spread,
     load_sem, send1, recv1, sendz, recvz_sem, send2, recv2, send3, recv3,
 ):
     nx, nz, nt, ny, nr, nv, nb, chunk = dims
@@ -41,10 +42,15 @@
     rows = fields.shape[0]
 
     load_f = pltpu.make_async_copy(fields_hbm, fields, load_sem.at[0])
-    load_v = pltpu.make_async_copy(vectors_hbm, vectors, load_sem.at[1])
-    load_o = pltpu.make_async_copy(ops_hbm, ops, load_sem.at[2])
+    pieces = [pl.ds(c * chunk, chunk) for c in range(vectors.shape[0] // chunk)]
+    load_v = [
+        pltpu.make_async_copy(vectors_hbm.at[part], vectors.at[part], load_sem.at[2 + c])
+        for c, part in enumerate(pieces)
+    ]
+    load_o = pltpu.make_async_copy(ops_hbm, ops, load_sem.at[1])
     load_f.start()
-    load_v.start()
+    for load in load_v:
+        load.start()
     load_o.start()
 
     barrier = pltpu.get_barrier_semaphore()
@@ -59,19 +65,13 @@
     j = lax.broadcasted_iota(jnp.int32, (vec_rows, 128), 1)
     lane_of = ((i >> shift) & 3) * nv + (i >> (shift + 2))
     fold[...] = jnp.where(lane_of == j, 1.0, 0.0).astype(BF16)
-    i = lax.broadcasted_iota(jnp.int32, (128, vec_rows), 1)
-    j = lax.broadcasted_iota(jnp.int32, (128, vec_rows), 0)
-    lane_of = ((i >> shift) & 3) * nv + (i >> (shift + 2))
-    spread[...] = jnp.where(lane_of == j, 1.0, 0.0).astype(BF16)
-
     load_f.wait()
-    load_v.wait()
 
     mask = same_block(rows, chunk, 2 * nb)
     left = fields[...]
     total = jnp.zeros((rows, 128), F32)
-    for c in range(vec_rows // chunk):
-        part = pl.ds(c * chunk, chunk)
+    for load, part in zip(load_v, pieces):
+        load.wait()
         grid = jnp.where(mask, dot(left, vectors[part, :], NT), 0.0)
         high = grid.astype(BF16)
         low = (grid - high.astype(F32)).astype(BF16)
@@ -88,11 +88,11 @@
         ext[nx + 1, r * ny:(r + 1) * ny, :] = coarse[:ny]
 
     pl.semaphore_wait(barrier, 3 * nx - 1)
-    sends = []
+    sends_x, sends_z = [], []
     for d in range(nx):
         other = lax.rem(me + d, nx)
         for side, plane in ((1, up), (0, down)):
-            sends.append(
+            sends_z.append(
                 pltpu.make_async_remote_copy(
                     src_ref=ext.at[other + 1],
                     dst_ref=recvz.at[side, me],
@@ -102,9 +102,9 @@
                     device_id_type=MESH,
                 )
             )
-            sends[-1].start()
+            sends_z[-1].start()
         if d > 0:
-            sends.append(
+            sends_x.append(
                 pltpu.make_async_remote_copy(
                     src_ref=ext.at[pl.ds(other, 3)],
                     dst_ref=recv.at[me],
@@ -114,19 +114,23 @@
                     device_id_type=MESH,
                 )
             )
-            sends[-1].start()
+            sends_x[-1].start()
     recv[pl.ds(me, 1)] = ext[pl.ds(me, 3)][None]
+
+    i = lax.broadcasted_iota(jnp.int32, (128, vec_rows), 1)
+    j = lax.broadcasted_iota(jnp.int32, (128, vec_rows), 0)
+    lane_of = ((i >> shift) & 3) * nv + (i >> (shift + 2))
+    spread[...] = jnp.where(lane_of == j, 1.0, 0.0).astype(BF16)
 
     load_o.wait()
     lane = lax.broadcasted_iota(jnp.int32, (64, 128), 1)
     sign64 = jnp.where(lane < 64, 1.0, -1.0)
     for t in range(nt):
         for y in range(ny):
-            for m in range(9):
+            for place, m in enumerate(ORDER):
                 a = ops[t * ny + y, m].astype(F32)
-                cols = pl.ds(m * 128, 128)
-                matrix[t, y * 128:y * 128 + 64, cols] = (a * sign64).astype(BF16)
-                matrix[t, y * 128 + 64:y * 128 + 128, cols] = pltpu.roll(a, 64, 1).astype(BF16)
+                both = jnp.concatenate([a * sign64, pltpu.roll(a, 64, 1)], axis=0)
+                matrix[t, place * 128:(place + 1) * 128, y * 128:(y + 1) * 128] = both.T.astype(BF16)
 
     site = lax.broadcasted_iota(jnp.int32, (nr * ny, 128), 0)
 
@@ -138,26 +142,33 @@
                 pieces.append(v[row:row + 1])
         return jnp.concatenate(pieces, axis=0)
 
-    def apply(own, xp, xm, zp, zm):
+    def product(t, first, terms):
+        around = jnp.concatenate(terms, axis=1).astype(BF16)
+        return dot(around, matrix[t, first * 128:(first + len(terms)) * 128, :], NN)
+
+    def near(own):
+        return [
+            product(
+                t,
+                0,
+                [own[t], roll_y(own[t], 1), roll_y(own[t], -1), own[(t + 1) % nt], own[(t - 1) % nt]],
+            )
+            for t in range(nt)
+        ]
+
+    def beside(total, first, plus, minus):
+        return [total[t] + product(t, first, [plus[t], minus[t]]) for t in range(nt)]
+
+    def picked(total):
         results = []
         for t in range(nt):
-            v = own[t]
-            yp, ym = roll_y(v, 1), roll_y(v, -1)
-            around = jnp.concatenate(
-                [v, xp[t], xm[t], yp, ym, zp[t], zm[t], own[(t + 1) % nt], own[(t - 1) % nt]],
-                axis=1,
-            )
-            product = dot(around.astype(BF16), matrix[t], NT)
-            value = product[:, :128]
+            value = total[t][:, :128]
             for y in range(1, ny):
                 value = jnp.where(
-                    lax.rem(site, ny) == y, product[:, y * 128:(y + 1) * 128], value
+                    lax.rem(site, ny) == y, total[t][:, y * 128:(y + 1) * 128], value
                 )
             results.append(value.astype(BF16).astype(F32))
         return results
-
-    for copy in sends:
-        copy.wait_recv()
 
     def summed(load):
         results = []
@@ -168,19 +179,21 @@
             results.append(value.astype(BF16).astype(F32))
         return results
 
-    applied = apply(
-        summed(lambda s: recv[s, 1]),
-        summed(lambda s: recv[s, 2]),
-        summed(lambda s: recv[s, 0]),
-        summed(lambda s: recvz[0, s]),
-        summed(lambda s: recvz[1, s]),
+    for copy in sends_x:
+        copy.wait_recv()
+    total = near(summed(lambda s: recv[s, 1]))
+    total = beside(total, 5, summed(lambda s: recv[s, 2]), summed(lambda s: recv[s, 0]))
+    for copy in sends_z:
+        copy.wait_recv()
+    applied = picked(
+        beside(total, 7, summed(lambda s: recvz[0, s]), summed(lambda s: recvz[1, s]))
     )
     for t in range(nt):
         mine[t] = applied[t]
 
     right = lax.rem(me + 1, nx)
     left_x = lax.rem(me + nx - 1, nx)
-    places = ((1, (right, z)), (0, (left_x, z)), (3, (me, up)), (2, (me, down)))
+    places = ((3, (me, up)), (2, (me, down)), (1, (right, z)), (0, (left_x, z)))
     round2 = []
     for slot, place in places:
         round2.append(
@@ -194,13 +207,14 @@
             )
         )
         round2[-1].start()
-    for copy in sends:
-        copy.wait_send()
-    for copy in round2:
-        copy.wait_recv()
-    twice = apply(
-        applied, *[[halo[slot, t] for t in range(nt)] for slot in range(4)]
-    )
+    total = near(applied)
+    arrived = lambda slot: [halo[slot, t] for t in range(nt)]
+    for copy in round2[2:]:
+        copy.wait_recv()
+    total = beside(total, 5, arrived(0), arrived(1))
+    for copy in round2[:2]:
+        copy.wait_recv()
+    twice = picked(beside(total, 7, arrived(2), arrived(3)))
     for t in range(nt):
         final[t] = twice[t]
 
@@ -219,21 +233,20 @@
         )
         round3[-1].start()
     gath[pl.ds(me, 1)] = final[pl.ds(me // TSITES, 1)]
-    for copy in round2:
+    for copy in sends_x + sends_z + round2:
         copy.wait_send()
     for copy in round3:
         copy.wait_recv()
 
-    pieces = []
+    mixings = []
     for r in range(nr):
         row = jnp.concatenate([gath[x, r * ny:(r + 1) * ny, :] for x in range(nx)], axis=0)
         real = sign * row
         imag = pltpu.roll(row, 64, 1)
-        pieces += [real, real, imag, imag]
-    mixing = jnp.concatenate(pieces, axis=0).astype(BF16)
+        mixings += [real, real, imag, imag]
+    mixing = jnp.concatenate(mixings, axis=0).astype(BF16)
     result = None
-    for c in range(vec_rows // chunk):
-        part = pl.ds(c * chunk, chunk)
+    for part in pieces:
         weights = jnp.where(mask, dot(mixing, spread[:, part], NN), 0.0).astype(BF16)
         term = dot(weights, vectors[part, :], NN)
         result = term if result is None else result + term
@@ -251,11 +264,13 @@
     nb, width = null_vectors.shape[-2:]
     vec_rows = nv * 4 * nb
     rows = nr * 4 * nb
+    chunk = vec_rows // 4
     message = (nr * ny, 128)
     dma = pltpu.SemaphoreType.DMA
+    vectors = null_vectors.reshape(vec_rows, width)
     out = pl.pallas_call(
-        functools.partial(kernel, (nx, nz, nt, ny, nr, nv, nb, min(vec_rows, 1024))),
-        out_shape=jax.ShapeDtypeStruct((rows, width), F32),
+        functools.partial(kernel, (nx, nz, nt, ny, nr, nv, nb, chunk)),
+        out_shape=pltpu.VMEM((rows, width), F32),
         in_specs=[pl.BlockSpec(memory_space=pl.ANY)] * 3,
         out_specs=pl.BlockSpec(memory_space=pltpu.VMEM),
         scratch_shapes=[
@@ -263,16 +278,16 @@
             pltpu.VMEM((vec_rows, width), BF16),
             pltpu.VMEM((nt * ny, 9, 64, 128), BF16),
             pltpu.VMEM((vec_rows, 128), BF16),
-            pltpu.VMEM((128, vec_rows), BF16),
             pltpu.VMEM((nx + 2,) + message, F32),
-            pltpu.VMEM((nt, ny * 128, 9 * 128), BF16),
+            pltpu.VMEM((nt, 9 * 128, ny * 128), BF16),
             pltpu.VMEM((nx, 3) + message, F32),
             pltpu.VMEM((2, nx) + message, F32),
             pltpu.VMEM((nt,) + message, F32),
             pltpu.VMEM((4, nt) + message, F32),
             pltpu.VMEM((nt,) + message, F32),
             pltpu.VMEM((nx,) + message, F32),
-            dma((3,)),
+            pltpu.VMEM((128, vec_rows), BF16),
+            dma((2 + vec_rows // chunk,)),
             dma((nx,)),
             dma((nx,)),
             dma((2, nx)),
@@ -283,11 +298,11 @@
             dma((nx,)),
         ],
         compiler_params=pltpu.CompilerParams(
-            collective_id=0, has_side_effects=True, vmem_limit_bytes=40 * 1024 * 1024
+            collective_id=0, has_side_effects=True, vmem_limit_bytes=62 * 1024 * 1024
         ),
     )(
         right_sides.reshape(rows, width),
-        null_vectors.reshape(vec_rows, width),
+        vectors,
         coarse_op.reshape((nt * ny,) + coarse_op.shape[4:]),
     )
     return out.reshape(right_sides.shape)

time: 23.6 us -> 20.1 us (0.85)
  local copies, waits for them, and re-layouts: 3.53 us -> 0.64 us
  Pallas kernels: 19.8 us -> 19.3 us
    unnamed x7 -> x1, local copies, waits for them, and re-layouts: 3.53 us -> 0.64 us
    pallas_call x1, Pallas kernels: 19.8 us -> 19.3 us  [per_device(): pl.pallas_call(functools.partial(kernel, (nx, nz, nt, ny, nr, nv, nb, chu...]
where the time goes in v2:
time: 20.1 us; the launch traced here: 20 us
  Pallas kernels  19.3 us (96%)
  local copies, waits for them, and re-layouts  0.64 us (3%)
    pallas_call x1, Pallas kernels, per_device(): pl.pallas_call(functools.partial(kernel, (nx, nz, nt, ny, nr, nv, nb, chu...  19.3 us
    unnamed x1, local copies, waits for them, and re-layouts  0.64 us

profile of v2, /device:TPU:0, one launch (start us, length us, event | category | flops | bytes accessed | tf_op | source)
XLA Modules:
  0.0 20.0 jit_solution(12042524683030169398)
XLA Ops:
  0.0 19.3 %shard_map.37 = f32[64,384]{1,0:T(8,128)S(1)} custom-call(bf16[64,384]{1,0:T(8,128)(2,1)} %bitcast.9, bf16[1024,384]{1,0:T(8,128)(2,1)} %bitcast.7, bf16[2,9,64,128]{3,2,1,0:T(8,128)(2,1)} %bitcast.8), custom_call_target="tpu_custom_call" | custom-call | tf_op jit(solution)/shard_map/pallas_call | solution.py:271
  19.3 0.6 %copy.6 = f32[2,2,2,1,1,8,384]{6,5,4,3,2,1,0:T(8,128)} copy(f32[2,2,2,1,1,8,384]{6,5,4,3,2,1,0:T(8,128)S(1)} %bitcast.6) | data formatting | bytes 196608

commit v3 on v2

--- a/solution.py
+++ b/solution.py
@@ -28,7 +28,7 @@
 
 def kernel(
     dims, fields_hbm, vectors_hbm, ops_hbm, out_ref,
-    fields, vectors, ops, fold, ext, matrix, recv, recvz, mine, halo, final, gath, spread,
+    fields, vectors, ops, ext, matrix, recv, recvz, mine, halo, final, gath, spread,
     load_sem, send1, recv1, sendz, recvz_sem, send2, recv2, send3, recv3,
 ):
     nx, nz, nt, ny, nr, nv, nb, chunk = dims
@@ -41,6 +41,14 @@
     vec_rows = vectors.shape[0]
     rows = fields.shape[0]
 
+    barrier = pltpu.get_barrier_semaphore()
+    for d in [*range(1, nx), 0]:
+        other = lax.rem(me + d, nx)
+        for plane in (up, down) if d == 0 else (up, down, z):
+            pl.semaphore_signal(
+                barrier, inc=1, device_id=(other, plane, col), device_id_type=MESH
+            )
+
     load_f = pltpu.make_async_copy(fields_hbm, fields, load_sem.at[0])
     pieces = [pl.ds(c * chunk, chunk) for c in range(vectors.shape[0] // chunk)]
     load_v = [
@@ -53,30 +61,26 @@
         load.start()
     load_o.start()
 
-    barrier = pltpu.get_barrier_semaphore()
-    for d in range(nx):
-        other = lax.rem(me + d, nx)
-        for plane in (up, down) if d == 0 else (up, down, z):
-            pl.semaphore_signal(
-                barrier, inc=1, device_id=(other, plane, col), device_id_type=MESH
-            )
-
-    i = lax.broadcasted_iota(jnp.int32, (vec_rows, 128), 0)
-    j = lax.broadcasted_iota(jnp.int32, (vec_rows, 128), 1)
+    i = lax.broadcasted_iota(jnp.int32, (128, vec_rows), 1)
+    j = lax.broadcasted_iota(jnp.int32, (128, vec_rows), 0)
     lane_of = ((i >> shift) & 3) * nv + (i >> (shift + 2))
-    fold[...] = jnp.where(lane_of == j, 1.0, 0.0).astype(BF16)
+    spread[...] = jnp.where(lane_of == j, 1.0, 0.0).astype(BF16)
+    lane = lax.broadcasted_iota(jnp.int32, (chunk, 2 * rows), 1)
+    high_half = lane < rows
+    mask_t = same_block(chunk, 2 * rows, 2 * nb)
+
     load_f.wait()
 
-    mask = same_block(rows, chunk, 2 * nb)
-    left = fields[...]
-    total = jnp.zeros((rows, 128), F32)
+    left = jnp.concatenate([fields[...], fields[...]], axis=0)
+    total = jnp.zeros((128, 2 * rows), F32)
     for load, part in zip(load_v, pieces):
         load.wait()
-        grid = jnp.where(mask, dot(left, vectors[part, :], NT), 0.0)
+        grid = jnp.where(mask_t, dot(vectors[part, :], left, NT), 0.0)
         high = grid.astype(BF16)
         low = (grid - high.astype(F32)).astype(BF16)
-        both = dot(jnp.concatenate([high, low], axis=0), fold[part, :], NN)
-        total = total + (both[:rows] + both[rows:])
+        total = total + dot(spread[:, part], jnp.where(high_half, high, low), NN)
+    total = total.T
+    total = total[:rows] + total[rows:]
     lane = lax.broadcasted_iota(jnp.int32, (nb, 128), 1)
     sign = jnp.where(lane < 64, 1.0, -1.0)
     for r in range(nr):
@@ -89,7 +93,7 @@
 
     pl.semaphore_wait(barrier, 3 * nx - 1)
     sends_x, sends_z = [], []
-    for d in range(nx):
+    for d in [*range(1, nx), 0]:
         other = lax.rem(me + d, nx)
         for side, plane in ((1, up), (0, down)):
             sends_z.append(
@@ -116,11 +120,6 @@
             )
             sends_x[-1].start()
     recv[pl.ds(me, 1)] = ext[pl.ds(me, 3)][None]
-
-    i = lax.broadcasted_iota(jnp.int32, (128, vec_rows), 1)
-    j = lax.broadcasted_iota(jnp.int32, (128, vec_rows), 0)
-    lane_of = ((i >> shift) & 3) * nv + (i >> (shift + 2))
-    spread[...] = jnp.where(lane_of == j, 1.0, 0.0).astype(BF16)
 
     load_o.wait()
     lane = lax.broadcasted_iota(jnp.int32, (64, 128), 1)
@@ -238,6 +237,7 @@
     for copy in round3:
         copy.wait_recv()
 
+    mask = same_block(rows, chunk, 2 * nb)
     mixings = []
     for r in range(nr):
         row = jnp.concatenate([gath[x, r * ny:(r + 1) * ny, :] for x in range(nx)], axis=0)
@@ -264,7 +264,7 @@
     nb, width = null_vectors.shape[-2:]
     vec_rows = nv * 4 * nb
     rows = nr * 4 * nb
-    chunk = vec_rows // 4
+    chunk = min(vec_rows // 2, 1024)
     message = (nr * ny, 128)
     dma = pltpu.SemaphoreType.DMA
     vectors = null_vectors.reshape(vec_rows, width)
@@ -277,7 +277,6 @@
             pltpu.VMEM((rows, width), BF16),
             pltpu.VMEM((vec_rows, width), BF16),
             pltpu.VMEM((nt * ny, 9, 64, 128), BF16),
-            pltpu.VMEM((vec_rows, 128), BF16),
             pltpu.VMEM((nx + 2,) + message, F32),
             pltpu.VMEM((nt, 9 * 128, ny * 128), BF16),
             pltpu.VMEM((nx, 3) + message, F32),

time: 20.1 us -> 19.9 us (0.990)
    pallas_call x1, Pallas kernels: 19.3 us -> 19.1 us  [per_device(): pl.pallas_call(functools.partial(kernel, (nx, nz, nt, ny, nr, nv, nb, chu...]
where the time goes in v3:
time: 19.9 us; the launch traced here: 19.7 us
  Pallas kernels  19.1 us (96%)
  local copies, waits for them, and re-layouts  0.64 us (3%)
    pallas_call x1, Pallas kernels, per_device(): pl.pallas_call(functools.partial(kernel, (nx, nz, nt, ny, nr, nv, nb, chu...  19.1 us
    unnamed x1, local copies, waits for them, and re-layouts  0.64 us

profile of v3, /device:TPU:0, one launch (start us, length us, event | category | flops | bytes accessed | tf_op | source)
XLA Modules:
  0.0 19.7 jit_solution(8587018691908985298)
XLA Ops:
  0.0 19.1 %shard_map.37 = f32[64,384]{1,0:T(8,128)S(1)} custom-call(bf16[64,384]{1,0:T(8,128)(2,1)} %bitcast.9, bf16[1024,384]{1,0:T(8,128)(2,1)} %bitcast.7, bf16[2,9,64,128]{3,2,1,0:T(8,128)(2,1)} %bitcast.8), custom_call_target="tpu_custom_call" | custom-call | tf_op jit(solution)/shard_map/pallas_call | solution.py:271
  19.1 0.6 %copy.6 = f32[2,2,2,1,1,8,384]{6,5,4,3,2,1,0:T(8,128)} copy(f32[2,2,2,1,1,8,384]{6,5,4,3,2,1,0:T(8,128)S(1)} %bitcast.6) | data formatting | bytes 196608

commit v4 on v3

--- a/solution.py
+++ b/solution.py
@@ -100,8 +100,8 @@
                 pltpu.make_async_remote_copy(
                     src_ref=ext.at[other + 1],
                     dst_ref=recvz.at[side, me],
-                    send_sem=sendz.at[side, d],
-                    recv_sem=recvz_sem.at[side, d],
+                    send_sem=sendz.at[0],
+                    recv_sem=recvz_sem.at[0],
                     device_id=(other, plane, col),
                     device_id_type=MESH,
                 )
@@ -112,8 +112,8 @@
                 pltpu.make_async_remote_copy(
                     src_ref=ext.at[pl.ds(other, 3)],
                     dst_ref=recv.at[me],
-                    send_sem=send1.at[d],
-                    recv_sem=recv1.at[d],
+                    send_sem=send1.at[0],
+                    recv_sem=recv1.at[0],
                     device_id=(other, z, col),
                     device_id_type=MESH,
                 )
@@ -178,12 +178,11 @@
             results.append(value.astype(BF16).astype(F32))
         return results
 
-    for copy in sends_x:
-        copy.wait_recv()
+    others = recv.at[pl.ds(0, nx - 1)]
+    pltpu.make_async_copy(others, others, recv1.at[0]).wait()
     total = near(summed(lambda s: recv[s, 1]))
     total = beside(total, 5, summed(lambda s: recv[s, 2]), summed(lambda s: recv[s, 0]))
-    for copy in sends_z:
-        copy.wait_recv()
+    pltpu.make_async_copy(recvz, recvz, recvz_sem.at[0]).wait()
     applied = picked(
         beside(total, 7, summed(lambda s: recvz[0, s]), summed(lambda s: recvz[1, s]))
     )
@@ -232,7 +231,9 @@
         )
         round3[-1].start()
     gath[pl.ds(me, 1)] = final[pl.ds(me // TSITES, 1)]
-    for copy in sends_x + sends_z + round2:
+    pltpu.make_async_copy(others, others, send1.at[0]).wait()
+    pltpu.make_async_copy(recvz, recvz, sendz.at[0]).wait()
+    for copy in round2:
         copy.wait_send()
     for copy in round3:
         copy.wait_recv()
@@ -287,10 +288,10 @@
             pltpu.VMEM((nx,) + message, F32),
             pltpu.VMEM((128, vec_rows), BF16),
             dma((2 + vec_rows // chunk,)),
-            dma((nx,)),
-            dma((nx,)),
-            dma((2, nx)),
-            dma((2, nx)),
+            dma((1,)),
+            dma((1,)),
+            dma((1,)),
+            dma((1,)),
             dma((4,)),
             dma((4,)),
             dma((nx,)),

time: 19.9 us -> 19.7 us (0.990)
  Pallas kernels: 19.1 us -> 18.9 us
where the time goes in v4:
time: 19.7 us; the launch traced here: 19.5 us
  Pallas kernels  18.9 us (96%)
  local copies, waits for them, and re-layouts  0.64 us (3%)
    pallas_call x1, Pallas kernels, per_device(): pl.pallas_call(functools.partial(kernel, (nx, nz, nt, ny, nr, nv, nb, chu...  18.9 us
    unnamed x1, local copies, waits for them, and re-layouts  0.64 us

profile of v4, /device:TPU:0, one launch (start us, length us, event | category | flops | bytes accessed | tf_op | source)
XLA Modules:
  0.0 19.5 jit_solution(13534565142077674542)
XLA Ops:
  0.0 18.9 %shard_map.37 = f32[64,384]{1,0:T(8,128)S(1)} custom-call(bf16[64,384]{1,0:T(8,128)(2,1)} %bitcast.9, bf16[1024,384]{1,0:T(8,128)(2,1)} %bitcast.7, bf16[2,9,64,128]{3,2,1,0:T(8,128)(2,1)} %bitcast.8), custom_call_target="tpu_custom_call" | custom-call | tf_op jit(solution)/shard_map/pallas_call | solution.py:272
  18.9 0.6 %copy.6 = f32[2,2,2,1,1,8,384]{6,5,4,3,2,1,0:T(8,128)} copy(f32[2,2,2,1,1,8,384]{6,5,4,3,2,1,0:T(8,128)S(1)} %bitcast.6) | data formatting | bytes 196608

commit v5 on v4

--- a/solution.py
+++ b/solution.py
@@ -198,8 +198,8 @@
             pltpu.make_async_remote_copy(
                 src_ref=mine,
                 dst_ref=halo.at[slot],
-                send_sem=send2.at[slot],
-                recv_sem=recv2.at[slot],
+                send_sem=send2.at[0],
+                recv_sem=recv2.at[slot // 2],
                 device_id=place + (col,),
                 device_id_type=MESH,
             )
@@ -207,11 +207,10 @@
         round2[-1].start()
     total = near(applied)
     arrived = lambda slot: [halo[slot, t] for t in range(nt)]
-    for copy in round2[2:]:
-        copy.wait_recv()
+    pair = halo.at[pl.ds(0, 2)]
+    pltpu.make_async_copy(pair, pair, recv2.at[0]).wait()
     total = beside(total, 5, arrived(0), arrived(1))
-    for copy in round2[:2]:
-        copy.wait_recv()
+    pltpu.make_async_copy(pair, pair, recv2.at[1]).wait()
     twice = picked(beside(total, 7, arrived(2), arrived(3)))
     for t in range(nt):
         final[t] = twice[t]
@@ -223,8 +222,8 @@
             pltpu.make_async_remote_copy(
                 src_ref=final.at[other // TSITES],
                 dst_ref=gath.at[me],
-                send_sem=send3.at[d],
-                recv_sem=recv3.at[d],
+                send_sem=send3.at[0],
+                recv_sem=recv3.at[0],
                 device_id=(other, z, col),
                 device_id_type=MESH,
             )
@@ -233,10 +232,9 @@
     gath[pl.ds(me, 1)] = final[pl.ds(me // TSITES, 1)]
     pltpu.make_async_copy(others, others, send1.at[0]).wait()
     pltpu.make_async_copy(recvz, recvz, sendz.at[0]).wait()
-    for copy in round2:
-        copy.wait_send()
-    for copy in round3:
-        copy.wait_recv()
+    pltpu.make_async_copy(halo, halo, send2.at[0]).wait()
+    rest = gath.at[pl.ds(0, nx - 1)]
+    pltpu.make_async_copy(rest, rest, recv3.at[0]).wait()
 
     mask = same_block(rows, chunk, 2 * nb)
     mixings = []
@@ -252,8 +250,7 @@
         term = dot(weights, vectors[part, :], NN)
         result = term if result is None else result + term
     out_ref[...] = result
-    for copy in round3:
-        copy.wait_send()
+    pltpu.make_async_copy(rest, rest, send3.at[0]).wait()
 
 
 def per_device(right_sides, null_vectors, coarse_op):
@@ -292,10 +289,10 @@
             dma((1,)),
             dma((1,)),
             dma((1,)),
-            dma((4,)),
-            dma((4,)),
-            dma((nx,)),
-            dma((nx,)),
+            dma((1,)),
+            dma((2,)),
+            dma((1,)),
+            dma((1,)),
         ],
         compiler_params=pltpu.CompilerParams(
             collective_id=0, has_side_effects=True, vmem_limit_bytes=62 * 1024 * 1024

time: 19.7 us -> 19.6 us (level)
  no operation moved by 1% of the time
where the time goes in v5:
time: 19.6 us; the launch traced here: 19.4 us
  Pallas kernels  18.8 us (96%)
  local copies, waits for them, and re-layouts  0.64 us (3%)
    pallas_call x1, Pallas kernels, per_device(): pl.pallas_call(functools.partial(kernel, (nx, nz, nt, ny, nr, nv, nb, chu...  18.8 us
    unnamed x1, local copies, waits for them, and re-layouts  0.64 us

profile of v5, /device:TPU:0, one launch (start us, length us, event | category | flops | bytes accessed | tf_op | source)
XLA Modules:
  0.0 19.4 jit_solution(3976067644197302804)
XLA Ops:
  0.0 18.8 %shard_map.37 = f32[64,384]{1,0:T(8,128)S(1)} custom-call(bf16[64,384]{1,0:T(8,128)(2,1)} %bitcast.9, bf16[1024,384]{1,0:T(8,128)(2,1)} %bitcast.7, bf16[2,9,64,128]{3,2,1,0:T(8,128)(2,1)} %bitcast.8), custom_call_target="tpu_custom_call" | custom-call | tf_op jit(solution)/shard_map/pallas_call | solution.py:269
  18.8 0.6 %copy.6 = f32[2,2,2,1,1,8,384]{6,5,4,3,2,1,0:T(8,128)} copy(f32[2,2,2,1,1,8,384]{6,5,4,3,2,1,0:T(8,128)S(1)} %bitcast.6) | data formatting | bytes 196608
